TPU v7x, 768 devices: a whole 4x8x12 slice. The times are simulated.
768 devices in a mesh: row: 64 (over x, y, core), col: 12 (over z).
Axes of the slice: x: 4, y: 8, z: 12, core: 2. Of those that a mesh axis runs over, the one named last changes fastest.
Arguments:
- features: bfloat16 [196608, 128], P(('row', 'col')), may hold values from -6 to 6
- send_rows: int32 [64, 12, 2048], P('row', 'col'), may hold values from 0 to 255, as said below
- send_count: int32 [64, 12, 64], P('row', 'col'), may hold values from 1 to 32, as said below
- tile_values: bfloat16 [64, 12, 64, 128, 128], P('row', 'col'), may hold values from -0.375 to 0.375
- tile_dst: int32 [64, 12, 64], P('row', 'col'), may hold values from 0 to 23, as said below
- tile_src: int32 [64, 12, 64], P('row', 'col'), may hold values from 0 to 15
- tile_count: int32 [64, 12], P('row', 'col'), may hold values from 1 to 64, as said below
- labels: int32 [196608], P(('row', 'col')), may hold values from 0 to 171
- train_mask: int32 [196608], P(('row', 'col')), may hold values from 0 to 1
- w_self1: bfloat16 [128, 512], replicated, may hold values from -0.5 to 0.5
- w_neigh1: bfloat16 [128, 512], replicated, may hold values from -0.5 to 0.5
- w_self2: bfloat16 [512, 172], replicated, may hold values from -0.25 to 0.25
- w_neigh2: bfloat16 [512, 172], replicated, may hold values from -0.25 to 0.25
Outputs:
- grad_self1: float32 [128, 512], replicated
- grad_neigh1: float32 [128, 512], replicated
- grad_self2: float32 [512, 172], replicated
- grad_neigh2: float32 [512, 172], replicated
- loss: float32 [], replicated
Inputs may be any that keep to these rules, and one draw needn't show every extreme that they name: `send_rows`: for each device and row peer the 32 entries name distinct local rows among the device's 256 nodes. `send_count`: some device sends exactly 32 live rows to some row peer. On each device the 64 tile slots have distinct pairs of tile_dst and tile_src. `tile_count`: some device has all 64 tiles live.
All inputs are finite; a program needn't handle non-finite values.
Results may differ from a plain program's by a relative error of at most 0.006.
The roundings to bfloat16 on the way count: a program that leaves them out, or rounds other values in their place, can miss the bound.
Values may be sent and summed in bfloat16 or wider, within the bound.
A program may use at most 64 MiB of HBM per device.

v0:
```python
import jax
import jax.numpy as jnp
from jax import lax
from jax.sharding import PartitionSpec as P


def trade_rows(outgoing):
    return lax.all_to_all(outgoing, "row", split_axis=0, concat_axis=0, tiled=True)


def place_rows(received, tile_blocks, source_block, dest_place):
    row_width = received.shape[1]
    block_size = tile_blocks.shape[-1]
    source_rows = received.reshape(received.shape[0] // block_size, block_size, row_width)[
        source_block
    ]
    products = jnp.einsum(
        "tij,tjw->tiw", tile_blocks, source_rows, preferred_element_type=jnp.float32
    )

    def term(row_start, row_count):
        placed = jnp.einsum("dt,tiw->diw", dest_place, products, precision=lax.Precision.HIGHEST)
        return placed.reshape(row_count, row_width)

    return term


def class_terms(logits, label_values, train_live):
    classes = logits.shape[1]
    log_total = jnp.log(jnp.sum(jnp.exp(logits), axis=-1))
    label_hits = (jnp.arange(classes, dtype=jnp.float32)[None, :] == label_values[:, None]).astype(
        jnp.float32
    )
    cross = log_total - jnp.sum(logits * label_hits, axis=-1)
    probability = jnp.exp(logits - log_total[:, None])
    grad_rows = (train_live[:, None] * (probability - label_hits)).astype(jnp.bfloat16)
    return (cross, grad_rows)


def shards(
    features,
    send_rows,
    send_count,
    tile_values,
    tile_dst,
    tile_src,
    tile_count,
    labels,
    train_mask,
    w_self1,
    w_neigh1,
    w_self2,
    w_neigh2,
):
    own_rows = features.shape[0]
    row_peers = lax.axis_size("row")
    sent_index = send_rows.reshape(-1)
    halo_rows = sent_index.shape[0]
    slot_cap = halo_rows // row_peers
    sent_valid = jnp.arange(halo_rows) % slot_cap < jnp.repeat(
        send_count.reshape(row_peers), slot_cap
    )
    tile_blocks = tile_values.reshape(tile_values.shape[2:])
    dest_block = tile_dst.reshape(-1)
    source_block = tile_src.reshape(-1)
    block_size = tile_blocks.shape[-1]
    group_rows = own_rows * lax.axis_size("col")
    tile_live = (jnp.arange(dest_block.shape[0]) < tile_count.reshape(())).astype(jnp.float32)
    dest_place = (jnp.arange(group_rows // block_size)[:, None] == dest_block[None, :]).astype(
        jnp.float32
    ) * tile_live[None, :]
    source_place = (jnp.arange(halo_rows // block_size)[:, None] == source_block[None, :]).astype(
        jnp.float32
    ) * tile_live[None, :]

    def outgoing_rows(node_rows):
        return jnp.where(sent_valid[:, None], node_rows[sent_index], jnp.zeros((), node_rows.dtype))

    term_first = place_rows(
        trade_rows(outgoing_rows(features)), tile_blocks, source_block, dest_place
    )
    agg1 = lax.psum_scatter(
        term_first(jnp.int32(0), lax.axis_size("col") * own_rows),
        "col",
        scatter_dimension=0,
        tiled=True,
    ).astype(jnp.bfloat16)
    pre1 = jnp.dot(features, w_self1, preferred_element_type=jnp.float32) + jnp.dot(
        agg1, w_neigh1, preferred_element_type=jnp.float32
    )
    hidden1 = jnp.maximum(pre1, 0.0).astype(jnp.bfloat16)
    self_logits = jnp.dot(hidden1, w_self2, preferred_element_type=jnp.float32)
    neigh2 = jnp.dot(hidden1, w_neigh2, preferred_element_type=jnp.float32).astype(jnp.bfloat16)
    term_second = place_rows(
        trade_rows(outgoing_rows(neigh2)), tile_blocks, source_block, dest_place
    )
    agg2 = lax.psum_scatter(
        term_second(jnp.int32(0), lax.axis_size("col") * own_rows),
        "col",
        scatter_dimension=0,
        tiled=True,
    ).astype(jnp.bfloat16)
    own_logits = self_logits + agg2.astype(jnp.float32)
    label_values = labels.astype(jnp.float32)
    train_live = train_mask.astype(jnp.float32)
    cross, grad_logits = class_terms(own_logits, label_values, train_live)
    loss_part = jnp.sum(train_live * cross)
    group_grads = lax.all_gather(grad_logits, "col", axis=0, tiled=True)
    count_part = jnp.sum(train_live)
    class_width = group_grads.shape[1]
    dest_rows = group_grads.reshape(group_rows // block_size, block_size, class_width)[dest_block]
    back_products = jnp.einsum(
        "tji,tjw->tiw", tile_blocks, dest_rows, preferred_element_type=jnp.float32
    )
    slot_grads = jnp.einsum(
        "st,tiw->siw", source_place, back_products, precision=lax.Precision.HIGHEST
    )
    slot_grads = slot_grads.reshape(halo_rows, class_width).astype(jnp.bfloat16)
    returned = trade_rows(slot_grads)
    owner_map = (
        (jnp.arange(own_rows)[:, None] == sent_index[None, :]) & sent_valid[None, :]
    ).astype(jnp.bfloat16)
    back_rows = jnp.dot(owner_map, returned, preferred_element_type=jnp.float32).astype(
        jnp.bfloat16
    )
    grad_hidden = jnp.einsum(
        "vc,hc->vh", grad_logits, w_self2, preferred_element_type=jnp.float32
    ) + jnp.einsum("vc,hc->vh", back_rows, w_neigh2, preferred_element_type=jnp.float32)
    grad_pre1 = jnp.where(pre1 > 0, grad_hidden, 0.0).astype(jnp.bfloat16)
    part_self1 = jnp.einsum("vf,vh->fh", features, grad_pre1, preferred_element_type=jnp.float32)
    part_neigh1 = jnp.einsum("vf,vh->fh", agg1, grad_pre1, preferred_element_type=jnp.float32)
    part_self2 = jnp.einsum("vh,vc->hc", hidden1, grad_logits, preferred_element_type=jnp.float32)
    part_neigh2 = jnp.einsum("vh,vc->hc", hidden1, back_rows, preferred_element_type=jnp.float32)
    summed_self1, summed_neigh1, summed_self2, summed_neigh2, loss_sum, node_count = lax.psum(
        (part_self1, part_neigh1, part_self2, part_neigh2, loss_part, count_part), ("row", "col")
    )
    node_count = jnp.maximum(node_count, 1.0)
    grad_scale = 1.0 / jnp.sqrt(node_count)
    return (
        summed_self1 * grad_scale,
        summed_neigh1 * grad_scale,
        summed_self2 * grad_scale,
        summed_neigh2 * grad_scale,
        loss_sum / node_count,
    )


def solution(mesh):
    in_specs = (
        P(("row", "col"), None),
        P("row", "col", None),
        P("row", "col", None),
        P("row", "col", None, None, None),
        P("row", "col", None),
        P("row", "col", None),
        P("row", "col"),
        P(("row", "col")),
        P(("row", "col")),
        P(),
        P(),
        P(),
        P(),
    )
    out_specs = (P(), P(), P(), P(), P())
    return jax.shard_map(shards, mesh=mesh, in_specs=in_specs, out_specs=out_specs, check_vma=False)
```

profile of v0, /device:TPU:1, one launch (start us, length us, event | category | flops | bytes accessed | tf_op | source)
XLA Modules:
  0.0 855.7 jit_solution(16283510385018654259)
XLA Ops:
  8.8 6.5 gather_fusion
  15.3 1.1 broadcast_select_fusion.1
  16.4 14.6 %all-to-all-start = ((bf16[64,32,128]{2,1,0:T(8,128)(2,1)}), bf16[64,32,128]{2,1,0:T(8,128)(2,1)S(1)}, u32[]{:S(2)}, u32[]{:S(2)}) async-start(bf16[64,32,128]{2,1,0:T(8,128)(2,1)} %broadcast_select_fusion.1), calls=%async_computation | async-start | bytes 1048576 | tf_op jit(solution)/shard_map/all_to_all | solution.py:8
  31.7 16.6 %all-to-all-done = bf16[64,32,128]{2,1,0:T(8,128)(2,1)S(1)} async-done(((bf16[64,32,128]{2,1,0:T(8,128)(2,1)}), bf16[64,32,128]{2,1,0:T(8,128)(2,1)S(1)}, u32[]{:S(2)}, u32[]{:S(2)}) %all-to-all-start) | async-done | bytes 524320 | tf_op jit(solution)/shard_map/all_to_all | solution.py:8
  48.4 2.2 gather_fusion.1
  50.5 5.2 fusion.12
  55.7 5.4 copy.29
  61.1 3.9 fusion.6
  65.0 1.5 copy.22
  66.8 51.6 %reduce-scatter.3.cloned.1.call-done = f32[256,128]{1,0:T(8,128)} async-done(((f32[3072,128]{1,0:T(8,128)}), f32[256,128]{1,0:T(8,128)}) %reduce-scatter.3.cloned.1.call-update) | async-done | bytes 131088 | tf_op jit(solution)/shard_map/reduce_scatter | solution.py:82
  118.4 1.9 maximum_convert_fusion
  120.7 9.0 %gather_fusion.2 = bf16[2048,172]{1,0:T(8,128)(2,1)} fusion(bf16[256,172]{1,0:T(8,128)(2,1)S(1)} %copy.23, s32[2048]{0:T(1024)S(1)} %broadcast_clamp_fusion), kind=kCustom, calls=%fused_computation.2 | custom fusion | bytes 1417216 | tf_op jit(solution)/shard_map/gather | solution.py:77
  129.7 1.5 broadcast_select_fusion
  131.2 46.1 %all_to_all.21 = bf16[64,32,172]{2,1,0:T(8,128)(2,1)S(1)} all-to-all(bf16[64,32,172]{2,1,0:T(8,128)(2,1)S(1)} %broadcast_select_fusion), channel_id=1, replica_groups=mesh['row'=64,'col'=12] {'row'}, dimensions={0} | all-to-all | bytes 1409024 | tf_op jit(solution)/shard_map/all_to_all | solution.py:8
  177.3 2.8 gather_fusion.3
  180.1 3.5 fusion.10
  183.6 4.3 fusion.17
  188.0 1.7 copy.33
  190.4 47.9 %reduce-scatter.5.cloned.1.call-done = f32[256,172]{0,1:T(8,128)} async-done(((f32[3072,172]{0,1:T(8,128)}), f32[256,172]{0,1:T(8,128)}) %reduce-scatter.5.cloned.1.call-update) | async-done | bytes 176144 | tf_op jit(solution)/shard_map/reduce_scatter | solution.py:97
  238.3 1.2 select_reduce_fusion
  240.9 58.4 %all-gather.2.cloned.1.call-done = bf16[3072,172]{0,1:T(8,128)(2,1)} async-done(((bf16[256,172]{0,1:T(8,128)(2,1)}), bf16[3072,172]{0,1:T(8,128)(2,1)}) %all-gather.2.cloned.1.call-update) | async-done | bytes 1056784 | tf_op jit(solution)/shard_map/all_gather | solution.py:108
  299.2 1.4 copy.34
  301.0 2.5 gather_fusion.4
  303.5 3.4 fusion.8
  307.0 4.2 fusion.20
  311.2 1.5 copy.25
  312.7 17.9 %all-to-all-start.2 = ((bf16[64,32,172]{2,1,0:T(8,128)(2,1)}), bf16[64,32,172]{2,1,0:T(8,128)(2,1)}, u32[]{:S(2)}, u32[]{:S(2)}) async-start(bf16[64,32,172]{2,1,0:T(8,128)(2,1)} %bitcast.22), calls=%async_computation.4 | async-start | bytes 2097152 | tf_op jit(solution)/shard_map/all_to_all | solution.py:8
  331.8 1.2 fusion.62
  333.0 26.1 %all-to-all-done.2 = bf16[64,32,172]{2,1,0:T(8,128)(2,1)} async-done(((bf16[64,32,172]{2,1,0:T(8,128)(2,1)}), bf16[64,32,172]{2,1,0:T(8,128)(2,1)}, u32[]{:S(2)}, u32[]{:S(2)}) %all-to-all-start.2) | async-done | bytes 704544 | tf_op jit(solution)/shard_map/all_to_all | solution.py:8
  359.1 2.0 fusion.25
  364.3 106.5 %all-reduce = (f32[]{:T(128)}, f32[]{:T(128)}) all-reduce(f32[]{:T(128)} %get-tuple-element.18, f32[]{:T(128)} %get-tuple-element.17), channel_id=1, replica_groups=mesh['row'=64,'col'=12] {'row','col'}, use_global_device_ids=true, to_apply=%region_5.6 | all-reduce | flops 2 | bytes 16 | tf_op jit(solution)/shard_map/psum | solution.py:134
  472.0 372.3 %all-reduce.4.cloned.1.call-done = (f32[128,512]{0,1:T(8,128)}, f32[128,512]{0,1:T(8,128)}, f32[512,172]{0,1:T(8,128)}, f32[512,172]{0,1:T(8,128)}) async-done(((f32[128,512]{0,1:T(8,128)}, f32[128,512]{0,1:T(8,128)}, f32[512,172]{0,1:T(8,128)}, f32[512,172]{0,1:T(8,128)}), (f32[128,512]{0,1:T(8,128)}, f32[128,512]{0,1:T(8,128)}, f32[512,172]{0,1:T(8,128)}, ...) | async-done | bytes 1228816 | tf_op jit(solution)/shard_map/psum | solution.py:134
  (74 shorter events, 12.9 us)
Async XLA Ops:
  7.2 43.4 %copy-start = (bf16[1,1,64,128,128]{4,3,2,1,0:T(8,128)(2,1)S(1)}, bf16[1,1,64,128,128]{4,3,2,1,0:T(8,128)(2,1)}, u32[]{:S(2)}) copy-start(bf16[1,1,64,128,128]{4,3,2,1,0:T(8,128)(2,1)} %param.16) | copy-start | bytes 6291460
  8.8 22.9 %copy-start.17 = (s32[1,1,64]{2,1,0:T(1,128)S(1)}, s32[1,1,64]{2,1,0:T(1,128)}, u32[]{:S(2)}) copy-start(s32[1,1,64]{2,1,0:T(1,128)} %param.18) | copy-start | bytes 772
  16.4 31.9 %all-to-all-start = ((bf16[64,32,128]{2,1,0:T(8,128)(2,1)}), bf16[64,32,128]{2,1,0:T(8,128)(2,1)S(1)}, u32[]{:S(2)}, u32[]{:S(2)}) async-start(bf16[64,32,128]{2,1,0:T(8,128)(2,1)} %broadcast_select_fusion.1), calls=%async_computation | async-start | bytes 1048576 | tf_op jit(solution)/shard_map/all_to_all | solution.py:8
  31.0 87.4 %reduce-scatter.3.cloned.1.call-start = ((), (), s32[]{:S(2)}) async-start(), calls=%async_computation.5 | async-start | bytes 1703936 | tf_op jit(solution)/shard_map/reduce_scatter | solution.py:82
  55.7 5.4 copy-start.14
  65.0 1.6 copy-start.1
  65.0 1.6 copy-start.11
  65.0 53.4 %copy-start.10 = (bf16[128,512]{1,0:T(8,128)(2,1)S(1)}, bf16[128,512]{1,0:T(8,128)(2,1)}, u32[]{:S(2)}) copy-start(bf16[128,512]{1,0:T(8,128)(2,1)} %param.23) | copy-start | bytes 393220
  66.5 53.8 %copy-start.4 = (bf16[512,172]{0,1:T(8,128)(2,1)S(1)}, bf16[512,172]{0,1:T(8,128)(2,1)}, u32[]{:S(2)}) copy-start(bf16[512,172]{0,1:T(8,128)(2,1)} %param.25) | copy-start | bytes 528388
  66.5 171.8 %reduce-scatter.5.cloned.1.call-start = ((), (), s32[]{:S(2)}) async-start(), calls=%async_computation.6 | async-start | bytes 2342912 | tf_op jit(solution)/shard_map/reduce_scatter | solution.py:97
  189.7 0.7 copy-start.16
  189.7 0.7 copy-start.13
  189.7 48.6 %copy-start.6 = (bf16[512,172]{0,1:T(8,128)(2,1)S(1)}, bf16[512,172]{0,1:T(8,128)(2,1)}, u32[]{:S(2)}) copy-start(bf16[512,172]{0,1:T(8,128)(2,1)} %param.24) | copy-start | bytes 528388
  189.7 109.5 %all-gather.2.cloned.1.call-start = ((), (), s32[]{:S(2)}) async-start(), calls=%async_computation.7 | async-start | bytes 1171456 | tf_op jit(solution)/shard_map/all_gather | solution.py:108
  311.2 19.4 %copy-start.15 = (s32[1,1,64]{2,1,0:T(1,128)S(1)}, s32[1,1,64]{2,1,0:T(1,128)}, u32[]{:S(2)}) copy-start(s32[1,1,64]{2,1,0:T(1,128)} %param.15) | copy-start | bytes 772
  311.2 19.6 %copy-start.3 = (bf16[256,172]{0,1:T(8,128)(2,1)S(1)}, bf16[256,172]{0,1:T(8,128)(2,1)}, u32[]{:S(2)}) copy-start(bf16[256,172]{0,1:T(8,128)(2,1)} %multiply_convert_fusion) | copy-start | bytes 264196
  312.7 46.4 %copy-start.12 = (s32[1,1,2048]{2,1,0:T(1,128)S(1)}, s32[1,1,2048]{2,1,0:T(1,128)}, u32[]{:S(2)}) copy-start(s32[1,1,2048]{2,1,0:T(1,128)} %param.14) | copy-start | bytes 24580
  312.7 46.3 %all-to-all-start.2 = ((bf16[64,32,172]{2,1,0:T(8,128)(2,1)}), bf16[64,32,172]{2,1,0:T(8,128)(2,1)}, u32[]{:S(2)}, u32[]{:S(2)}) async-start(bf16[64,32,172]{2,1,0:T(8,128)(2,1)} %bitcast.22), calls=%async_computation.4 | async-start | bytes 2097152 | tf_op jit(solution)/shard_map/all_to_all | solution.py:8
  330.6 513.7 %all-reduce.4.cloned.1.call-start = ((), (), s32[]{:S(2)}) async-start(), calls=%async_computation.8 | async-start | bytes 2490368 | tf_op jit(solution)/shard_map/psum | solution.py:134
  330.8 31.2 %copy-start.2 = (f32[256,512]{1,0:T(8,128)S(1)}, f32[256,512]{1,0:T(8,128)}, u32[]{:S(2)}) copy-start(f32[256,512]{1,0:T(8,128)} %get-tuple-element.27) | copy-start | bytes 1572868
  359.1 3.0 copy-start.5
  359.1 4.2 copy-start.7
  844.3 2.8 copy-start.8
  844.3 2.8 copy-start.9
Sparse Core Ops, SparseCore 0:
  66.6 51.7 reduce-scatter.2
  189.9 48.4 reduce-scatter.4
  241.2 58.0 all-gather.1
  364.4 479.8 all-reduce.3
where the time goes:
time: 857 us; the launch traced here: 856 us
  waiting for transfers between devices  573 us (67%)
  blocking collectives  153 us (18%)
  local copies, waits for them, and re-layouts  37.3 us (4%)
  matrix products  35.3 us (4%)
  starting transfers between devices  32.8 us (4%)
  between operations  17.1 us (2%)
    psum x1, waiting for transfers between devices, shards(): lax.psum((part_self1, part_neigh1, part_self2, part_neigh2, loss_part, co...  372 us
    psum x1, blocking collectives, shards(): lax.psum((part_self1, part_neigh1, part_self2, part_neigh2, loss_part, co...  107 us
    all_gather x1, waiting for transfers between devices, shards(): group_grads = lax.all_gather(grad_logits, 'col', axis=0, tiled=True)  58.4 us
    reduce_scatter x1, waiting for transfers between devices, shards(): lax.psum_scatter(term_first(jnp.int32(0), lax.axis_size('col') * own_rows...  51.6 us
    reduce_scatter x1, waiting for transfers between devices, shards(): lax.psum_scatter(term_second(jnp.int32(0), lax.axis_size('col') * own_row...  47.9 us
    all_to_all x1, blocking collectives, trade_rows(): lax.all_to_all(outgoing, 'row', split_axis=0, concat_axis=0, tiled=True)  46.1 us
    all_to_all x2, waiting for transfers between devices, trade_rows(): lax.all_to_all(outgoing, 'row', split_axis=0, concat_axis=0, tiled=True)  42.7 us
    all_to_all x2, starting transfers between devices, trade_rows(): lax.all_to_all(outgoing, 'row', split_axis=0, concat_axis=0, tiled=True)  32.4 us
  transfers between devices with their start and end apart: 6, of which 6 were waited for; matrix products, arithmetic and copies ran while one was open for 0% of the time, Pallas kernels for 0%

commit v1 on v0

v1 whole, which is shorter than its diff:
```python
import jax
import jax.numpy as jnp
from jax import lax
from jax.experimental import pallas as pl
from jax.experimental.pallas import tpu as pltpu
from jax.sharding import PartitionSpec as P

MESH = pl.DeviceIdType.MESH
f32, bf16, i32 = jnp.float32, jnp.bfloat16, jnp.int32

NX, NY = 4, 8
NR, NZ = 64, 12
CLASSES = 172
TAIL = CLASSES - 128
UP, DOWN = 6, 5


def mm(a, b):
    return jnp.dot(a, b, preferred_element_type=f32)


def mm_t(a, b):
    return lax.dot_general(a, b, (((0,), (0,)), ((), ())), preferred_element_type=f32)


def mm_nt(a, b):
    return lax.dot_general(a, b, (((1,), (1,)), ((), ())), preferred_element_type=f32)


def lanes_of(shape):
    return lax.broadcasted_iota(i32, shape, len(shape) - 1)


def split3(value):
    high = value.astype(bf16).astype(f32)
    middle = (value - high).astype(bf16).astype(f32)
    return high, middle, value - high - middle


def put_scalars(rows, loss, count):
    lanes = lanes_of(rows.shape)
    first = lax.broadcasted_iota(i32, rows.shape, len(rows.shape) - 2) == 0
    for at, part in enumerate(split3(loss) + split3(count)):
        rows = jnp.where(first & (lanes == TAIL + at), part.reshape((1,) * len(rows.shape)), rows)
    return rows


def get_scalars(rows):
    lanes = lanes_of(rows.shape)
    first = lax.broadcasted_iota(i32, rows.shape, 0) == 0

    def total(low):
        live = first & (lanes >= low) & (lanes < low + 3)
        picked = jnp.where(live, rows, 0.0)
        return jnp.sum(jnp.sum(picked, axis=1, keepdims=True), axis=0, keepdims=True)

    return total(TAIL), total(TAIL + 3)


def half_turn(rows):
    return pltpu.roll(rows, 64, axis=1)


def kernel(
    cell, feat, rows, cnt, tiles_hbm, lab, mask, ws1, wn1, w2,
    g1, g2, g3, g4, loss_out,
    tiles, dense, pick, s1, r1, s2, r2, s3, r3, wide,
    up_s, up_r, dn_s, dn_r, up2_s, up2_r, dn2_s, dn2_r, gbuf, st,
    pre1, hidden, agg1, gl, sl, neigh, back, mine, pair_r, hs, hr, zs, zr, fin,
    tile_sem, a1, a2, a3, us, ur, ds, dr, us2, ur2, ds2, dr2, gus, gur, gds, gdr,
    pair_sem, hsem, zsem, fsem, pair2_sem,
):
    me = lax.axis_index("row")
    z = lax.axis_index("col")
    core, chip = lax.rem(me, 2), me // 2
    x, y = chip // NY, lax.rem(chip, NY)
    above, below = lax.rem(z + 1, NZ), lax.rem(z + NZ - 1, NZ)
    partner = chip * 2 + 1 - core

    tile_copy = pltpu.make_async_copy(tiles_hbm, tiles.at[pl.ds(0, 64)], tile_sem)
    tile_copy.start()

    barrier = pltpu.get_barrier_semaphore()

    def greet_row(k, c):
        pl.semaphore_signal(barrier, inc=1, device_id=(lax.rem(me + k, NR), z), device_id_type=MESH)
        return c

    def greet_col(k, c):
        pl.semaphore_signal(barrier, inc=1, device_id=(me, lax.rem(z + k, NZ)), device_id_type=MESH)
        return c

    lax.fori_loop(1, NR, greet_row, 0)
    lax.fori_loop(1, NZ, greet_col, 0)

    peer_of = lax.broadcasted_iota(i32, (NR, 2048), 1) // 32 == lax.broadcasted_iota(i32, (NR, 2048), 0)
    counts = jnp.broadcast_to(cnt[...].astype(f32), (8, NR)).astype(bf16)
    live_rows = mm(counts, peer_of.astype(f32).astype(bf16))[0:1]
    place = lax.rem(lax.broadcasted_iota(i32, (1, 2048), 1), 32).astype(f32)
    wanted = jnp.where(place < live_rows, rows[...].astype(f32), -1.0)
    tall = jnp.transpose(jnp.broadcast_to(wanted, (128, 2048)))
    node = lax.broadcasted_iota(i32, (2048, 128), 1).astype(f32)
    pick[:, 0:128] = (tall == node).astype(f32).astype(bf16)
    pick[:, 128:256] = (tall == node + 128.0).astype(f32).astype(bf16)

    pl.semaphore_wait(barrier, NR - 1 + NZ - 1)

    def group_of(dx):
        return lax.rem(x + dx, NX)

    def send_group(dx, src, dst, sem):
        def one(i, c):
            py = lax.rem(y + lax.rem(i // 2 * 3, NY), NY)
            peer = (group_of(dx) * NY + py) * 2 + lax.rem(core + lax.rem(i, 2), 2)
            pltpu.make_async_remote_copy(
                src_ref=src.at[peer], dst_ref=dst.at[me], send_sem=sem.at[0], recv_sem=sem.at[1],
                device_id=(peer, z), device_id_type=MESH,
            ).start()
            return c

        lax.fori_loop(1 if dx == 0 else 0, 16, one, 0)

    def all_of(src, dst, sem, number):
        return pltpu.make_async_remote_copy(
            src_ref=src.at[pl.ds(0, number)], dst_ref=dst.at[pl.ds(0, number)],
            send_sem=sem.at[0], recv_sem=sem.at[1], device_id=(partner, z), device_id_type=MESH,
        )

    def pack_group(dx, value, dst, scalars):
        first = group_of(dx) * 16
        dst[pl.ds(first, 16), 0:32, :] = value[:, 0:128].astype(bf16).reshape(16, 32, 128)
        tail = value[:, 128:256].reshape(16, 2, 16, 128)
        low, high = tail[:, 0], tail[:, 1]
        high = half_turn(high.reshape(256, 128)).reshape(16, 16, 128)
        both = low + high
        if scalars is not None:
            both = put_scalars(both, *scalars)
        dst[pl.ds(first, 16), 32:48, :] = both.astype(bf16)

    def unpack_rows(src):
        def one(i, c):
            part = pl.ds(i * 8, 8)
            wide[part, :, 0:128] = src[part, 0:32, :]
            tail = src[part, 32:48, :].astype(f32).reshape(128, 128)
            live = lanes_of((128, 128)) < TAIL
            low = jnp.where(live, tail, 0.0).astype(bf16)
            high = jnp.where(live, half_turn(tail), 0.0).astype(bf16)
            wide[part, 0:16, 128:256] = low.reshape(8, 16, 128)
            wide[part, 16:32, 128:256] = high.reshape(8, 16, 128)
            return c

        lax.fori_loop(0, 8, one, 0)

    order = (2, 1, 3, 0)
    for dx in order:
        at = pl.ds(pl.multiple_of(group_of(dx) * 512, 512), 512)
        block = mm(pick[at, :], feat[...]).astype(bf16)
        s1[pl.ds(group_of(dx) * 16, 16)] = block.reshape(16, 32, 128)
        send_group(dx, s1, r1, a1)
    r1[me] = s1[me]

    tile_copy.wait()
    tiles[64] = jnp.zeros((128, 128), bf16)

    def lay(d, c):
        for s in range(16):
            at = pl.ds(pl.multiple_of(d * 128, 128), 128)
            dense[at, s * 128 : (s + 1) * 128] = tiles[cell[d * 16 + s]]
        return c

    lax.fori_loop(0, 24, lay, 0)
    pre1[...] = mm(feat[...], ws1[...])
    up_r[0] = jnp.zeros(up_r.shape[1:], f32)
    dn_r[0] = jnp.zeros(dn_r.shape[1:], f32)
    up2_r[0] = jnp.zeros(up2_r.shape[1:], bf16)
    dn2_r[0] = jnp.zeros(dn2_r.shape[1:], bf16)

    def hop(src, dst, ssem, rsem, j, h, to):
        half = src.shape[1] // 2
        part = pl.ds(h * half, half)
        return pltpu.make_async_remote_copy(
            src_ref=src.at[j, part], dst_ref=dst.at[j + 1, part],
            send_sem=ssem.at[j, h], recv_sem=rsem.at[j, h], device_id=(me, to), device_id_type=MESH,
        )

    def ring_sum(chunk, ups, upr, dns, dnr, uss, urs, dss, drs):
        half = ups.shape[1] // 2

        def move(value, src, dst, ssem, rsem, j, to):
            for h in range(2):
                part = pl.ds(h * half, half)

                @pl.when(j > 0)
                def _():
                    hop(src, dst, ssem, rsem, j - 1, h, to).wait_recv()

                got = dst[j, part].astype(f32)
                src[j, part] = (value[h * half : (h + 1) * half] + got).astype(src.dtype)
                hop(src, dst, ssem, rsem, j, h, to).start()

        def step(j, c):
            high = chunk(lax.rem(z + UP - j, NZ))
            low = chunk(lax.rem(z + NZ - DOWN + j, NZ))
            move(high, ups, upr, uss, urs, j, above)
            move(low, dns, dnr, dss, drs, j, below)
            return c

        lax.fori_loop(0, DOWN, step, 0)
        move(chunk(above), ups, upr, uss, urs, UP - 1, above)
        own = chunk(z)
        for h in range(2):
            hop(dns, dnr, dss, drs, DOWN - 1, h, below).wait_recv()
        for h in range(2):
            hop(ups, upr, uss, urs, UP - 1, h, above).wait_recv()
        return own + dnr[DOWN].astype(f32) + upr[UP].astype(f32)

    def ring_sent(ups, upr, dns, dnr, uss, urs, dss, drs):
        def sent(j, c):
            for h in range(2):
                hop(ups, upr, uss, urs, j, h, above).wait_send()

                @pl.when(j < DOWN)
                def _():
                    hop(dns, dnr, dss, drs, j, h, below).wait_send()

            return c

        lax.fori_loop(0, UP, sent, 0)

    def block_rows(o):
        return dense[pl.ds(pl.multiple_of(o * 256, 256), 256), :]

    all_of(s1, r1, a1, NR - 1).wait_recv()

    def chunk1(o):
        return mm(block_rows(o), r1[...].reshape(2048, 128))

    ring1 = (up_s, up_r, dn_s, dn_r, us, ur, ds, dr)
    agg1[...] = ring_sum(chunk1, *ring1).astype(bf16)

    pre = pre1[...] + mm(agg1[...], wn1[...])
    pre1[...] = pre
    hidden[...] = jnp.maximum(pre, 0.0).astype(bf16)
    neigh[...] = mm(hidden[...], w2[:, 256:512]).astype(bf16)

    for dx in order:
        at = pl.ds(pl.multiple_of(group_of(dx) * 512, 512), 512)
        pack_group(dx, mm(pick[at, :], neigh[...]), s2, None)
        send_group(dx, s2, r2, a2)
    r2[me] = s2[me]
    sl[...] = mm(hidden[...], w2[:, 0:256])
    ring_sent(*ring1)
    all_of(s1, r1, a1, NR - 1).wait_send()
    all_of(s2, r2, a2, NR - 1).wait_recv()
    unpack_rows(r2)

    def pack_chunk(full):
        tail = full[:, 128:256]
        both = tail[0:128] + half_turn(tail[128:256])
        return jnp.concatenate([full[:, 0:128], both], axis=0)

    def unpack_chunk(packed):
        tail = packed[256:384]
        live = lanes_of((128, 128)) < TAIL
        low = jnp.where(live, tail, 0.0)
        high = jnp.where(live, half_turn(tail), 0.0)
        return jnp.concatenate([packed[0:256], jnp.concatenate([low, high], axis=0)], axis=1)

    def chunk2(o):
        return pack_chunk(mm(block_rows(o), wide[...].reshape(2048, 256)))

    ring2 = (up2_s, up2_r, dn2_s, dn2_r, us2, ur2, ds2, dr2)
    agg2 = unpack_chunk(ring_sum(chunk2, *ring2)).astype(bf16).astype(f32)

    logits = sl[...] + agg2
    lanes = lanes_of((256, 256))
    live = lanes < CLASSES

    def tall_of(ref):
        one = jnp.transpose(jnp.broadcast_to(ref[...].astype(f32), (128, 256)))
        return jnp.concatenate([one, one], axis=1)

    hit = lanes.astype(f32) == tall_of(lab)
    train = tall_of(mask)
    log_total = jnp.log(jnp.sum(jnp.where(live, jnp.exp(logits), 0.0), axis=1, keepdims=True))
    cross = log_total - jnp.sum(jnp.where(hit, logits, 0.0), axis=1, keepdims=True)
    prob = jnp.where(live, jnp.exp(logits - log_total), 0.0)
    grad = (train * (prob - hit.astype(f32))).astype(bf16)
    gl[...] = grad
    loss_part = jnp.sum(train[:, 0:1] * cross, axis=0, keepdims=True)
    count_part = jnp.sum(train[:, 0:1], axis=0, keepdims=True)

    packed = pack_chunk(grad.astype(f32))
    gbuf[z, 0:256] = packed[0:256].astype(bf16)
    gbuf[z, 256:384] = put_scalars(packed[256:384], loss_part, count_part).astype(bf16)

    def pass_on(owner, ssem, rsem, j, h, to):
        part = pl.ds(h * 192, 192)
        return pltpu.make_async_remote_copy(
            src_ref=gbuf.at[owner, part], dst_ref=gbuf.at[owner, part],
            send_sem=ssem.at[j, h], recv_sem=rsem.at[j, h], device_id=(me, to), device_id_type=MESH,
        )

    def up_hop(j, h):
        return pass_on(lax.rem(z + NZ - j, NZ), gus, gur, j, h, above)

    def down_hop(j, h):
        return pass_on(lax.rem(z + j, NZ), gds, gdr, j, h, below)

    def back_chunk(o):
        full = unpack_chunk(gbuf[o].astype(f32))
        return mm(jnp.transpose(full).astype(bf16), block_rows(o))

    for h in range(2):
        up_hop(0, h).start()
        down_hop(0, h).start()
    st[...] = back_chunk(z)

    def gather_step(j, c):
        for h in range(2):
            up_hop(j - 1, h).wait_recv()
            up_hop(j, h).start()
            down_hop(j - 1, h).wait_recv()

            @pl.when(j < DOWN)
            def _():
                down_hop(j, h).start()

        st[...] += back_chunk(lax.rem(z + NZ - j, NZ)) + back_chunk(lax.rem(z + j, NZ))
        return c

    lax.fori_loop(1, UP, gather_step, 0)
    for h in range(2):
        up_hop(UP - 1, h).wait_recv()
    st[...] += back_chunk(lax.rem(z + NZ - UP, NZ))
    col_sums = get_scalars(jnp.sum(gbuf[:, 256:272, :].astype(f32), axis=0))

    for dx in order:
        at = pl.ds(pl.multiple_of(group_of(dx) * 512, 512), 512)
        pack_group(dx, jnp.transpose(st[:, at]), s3, col_sums)
        send_group(dx, s3, r3, a3)
    r3[me] = s3[me]

    ring_sent(*ring2)

    def gather_sent(j, c):
        for h in range(2):
            up_hop(j, h).wait_send()

            @pl.when(j < DOWN)
            def _():
                down_hop(j, h).wait_send()

        return c

    lax.fori_loop(0, UP, gather_sent, 0)
    all_of(s2, r2, a2, NR - 1).wait_send()
    all_of(s3, r3, a3, NR - 1).wait_recv()
    unpack_rows(r3)
    loss_sum, node_count = get_scalars(jnp.sum(r3[:, 32:48, :].astype(f32), axis=0))

    back[...] = mm_t(pick[...], wide[...].reshape(2048, 256)).astype(bf16)

    grad_hidden = mm_nt(gl[...], w2[:, 0:256]) + mm_nt(back[...], w2[:, 256:512])
    grad_pre = jnp.where(pre1[...] > 0, grad_hidden, 0.0).astype(bf16)
    parts = (
        mm_t(feat[...], grad_pre),
        mm_t(agg1[...], grad_pre),
        mm_t(gl[...], hidden[...])[0:192],
        mm_t(back[...], hidden[...])[0:192],
        jnp.zeros((128, 512), f32),
    )
    for b in range(4):
        cut = jnp.concatenate([part[:, b * 128 : (b + 1) * 128] for part in parts], axis=0)
        mine[b * 16 : (b + 1) * 16] = cut.reshape(16, 48, 128)

    def to_pair(src, dst, sem, first_s, first_d):
        return pltpu.make_async_remote_copy(
            src_ref=src.at[pl.ds(first_s, 32)], dst_ref=dst.at[pl.ds(first_d, 32)],
            send_sem=sem.at[0], recv_sem=sem.at[1], device_id=(partner, z), device_id_type=MESH,
        )

    swap = to_pair(mine, pair_r, pair_sem, (1 - core) * 32, 0)
    swap.start()
    swap.wait_recv()
    hs[...] = (mine[pl.ds(core * 32, 32)] + pair_r[...]).astype(bf16)

    def plane_send(k, src, dst, at, sem):
        other = lax.rem(x + k // NY, NX) * NY + lax.rem(y + lax.rem(k * 3, NY), NY)
        source = src.at[other] if at is None else src.at[at]
        target = dst.at[chip] if at is None else dst.at[at]
        pltpu.make_async_remote_copy(
            src_ref=source, dst_ref=target, send_sem=sem.at[0], recv_sem=sem.at[1],
            device_id=(other * 2 + core, z), device_id_type=MESH,
        ).start()

    def scatter_one(k, c):
        plane_send(k, hs, hr, None, hsem)
        return c

    lax.fori_loop(1, 32, scatter_one, 0)
    hr[chip] = hs[chip]
    all_of(s3, r3, a3, NR - 1).wait_send()
    swap.wait_send()
    all_of(hs, hr, hsem, 31).wait_recv()
    zs[...] = jnp.sum(hr[...].astype(f32), axis=0).astype(bf16)

    def planes_one(k, c):
        pltpu.make_async_remote_copy(
            src_ref=zs, dst_ref=zr.at[z], send_sem=zsem.at[0], recv_sem=zsem.at[1],
            device_id=(me, lax.rem(z + k, NZ)), device_id_type=MESH,
        ).start()
        return c

    lax.fori_loop(1, NZ, planes_one, 0)
    zr[z] = zs[...]
    all_of(hs, hr, hsem, 31).wait_send()
    all_of(zr, zr, zsem, NZ - 1).wait_recv()
    piece = core * 32 + chip
    fin[piece] = jnp.sum(zr[...].astype(f32), axis=0).astype(bf16)

    def gather_one(k, c):
        plane_send(k, fin, fin, piece, fsem)
        return c

    lax.fori_loop(1, 32, gather_one, 0)
    all_of(zr, zr, zsem, NZ - 1).wait_send()
    all_of(fin, fin, fsem, 31).wait_recv()
    swap2 = to_pair(fin, fin, pair2_sem, core * 32, core * 32)
    swap2.start()

    node_count = jnp.maximum(node_count, 1.0)
    scale = 1.0 / jnp.sqrt(node_count)
    loss_out[...] = jnp.broadcast_to(loss_sum / node_count, (8, 128))
    swap2.wait_recv()
    for b in range(4):
        at = slice(b * 128, (b + 1) * 128)
        cut = fin[b * 16 : (b + 1) * 16].astype(f32).reshape(768, 128) * scale
        g1[:, at] = cut[0:128]
        g2[:, at] = cut[128:256]
        g3[at, :] = jnp.transpose(cut[256:512])[:, 0:CLASSES]
        g4[at, :] = jnp.transpose(cut[448:704])[:, 0:CLASSES]
    all_of(fin, fin, fsem, 31).wait_send()
    swap2.wait_send()


def shards(
    features, send_rows, send_count, tile_values, tile_dst, tile_src, tile_count,
    labels, train_mask, w_self1, w_neigh1, w_self2, w_neigh2,
):
    slots = jnp.arange(64, dtype=i32)
    where = tile_dst.reshape(1, 64) * 16 + tile_src.reshape(1, 64)
    lives = (jnp.arange(384, dtype=i32)[:, None] == where) & (slots < tile_count.reshape(()))[None, :]
    cell = jnp.min(jnp.where(lives, slots[None, :], 64), axis=1)
    fill = ((0, 0), (0, 256 - CLASSES))
    w2 = jnp.concatenate([jnp.pad(w_self2, fill), jnp.pad(w_neigh2, fill)], axis=1)
    vm = pl.BlockSpec(memory_space=pltpu.VMEM)
    sm = pl.BlockSpec(memory_space=pltpu.SMEM)
    V = pltpu.VMEM
    dma = pltpu.SemaphoreType.DMA
    out = pl.pallas_call(
        kernel,
        out_shape=[
            jax.ShapeDtypeStruct((128, 512), f32),
            jax.ShapeDtypeStruct((128, 512), f32),
            jax.ShapeDtypeStruct((512, CLASSES), f32),
            jax.ShapeDtypeStruct((512, CLASSES), f32),
            jax.ShapeDtypeStruct((8, 128), f32),
        ],
        in_specs=[sm, vm, vm, vm, pl.BlockSpec(memory_space=pl.ANY), vm, vm, vm, vm, vm],
        out_specs=[vm] * 5,
        scratch_shapes=[
            V((65, 128, 128), bf16),
            V((3072, 2048), bf16),
            V((2048, 256), bf16),
            V((64, 32, 128), bf16), V((64, 32, 128), bf16),
            V((64, 48, 128), bf16), V((64, 48, 128), bf16),
            V((64, 48, 128), bf16), V((64, 48, 128), bf16),
            V((64, 32, 256), bf16),
            V((UP, 256, 128), f32), V((UP + 1, 256, 128), f32),
            V((DOWN, 256, 128), f32), V((DOWN + 1, 256, 128), f32),
            V((UP, 384, 128), bf16), V((UP + 1, 384, 128), bf16),
            V((DOWN, 384, 128), bf16), V((DOWN + 1, 384, 128), bf16),
            V((NZ, 384, 128), bf16),
            V((256, 2048), f32),
            V((256, 512), f32),
            V((256, 512), bf16),
            V((256, 128), bf16),
            V((256, 256), bf16),
            V((256, 256), f32),
            V((256, 256), bf16),
            V((256, 256), bf16),
            V((64, 48, 128), f32), V((32, 48, 128), f32),
            V((32, 48, 128), bf16), V((32, 48, 128), bf16),
            V((48, 128), bf16), V((NZ, 48, 128), bf16),
            V((64, 48, 128), bf16),
            dma, dma((2,)), dma((2,)), dma((2,)),
            dma((UP, 2)), dma((UP, 2)), dma((DOWN, 2)), dma((DOWN, 2)),
            dma((UP, 2)), dma((UP, 2)), dma((DOWN, 2)), dma((DOWN, 2)),
            dma((UP, 2)), dma((UP, 2)), dma((DOWN, 2)), dma((DOWN, 2)),
            dma((2,)), dma((2,)), dma((2,)), dma((2,)), dma((2,)),
        ],
        compiler_params=pltpu.CompilerParams(
            collective_id=0, has_side_effects=True, vmem_limit_bytes=56 * 1024 * 1024
        ),
        name="sage_step",
    )(
        cell, features, send_rows.reshape(1, 2048), send_count.reshape(1, 64),
        tile_values.reshape(64, 128, 128), labels.reshape(1, 256), train_mask.reshape(1, 256),
        w_self1, w_neigh1, w2,
    )
    return (*out[:4], out[4][0, 0])


def solution(mesh):
    in_specs = (
        P(("row", "col"), None),
        P("row", "col", None),
        P("row", "col", None),
        P("row", "col", None, None, None),
        P("row", "col", None),
        P("row", "col", None),
        P("row", "col"),
        P(("row", "col")),
        P(("row", "col")),
        P(),
        P(),
        P(),
        P(),
    )
    out_specs = (P(), P(), P(), P(), P())
    return jax.shard_map(shards, mesh=mesh, in_specs=in_specs, out_specs=out_specs, check_vma=False)
```

time: 857 us -> 192 us (0.22)
  waiting for transfers between devices: 573 us -> 0 us
  Pallas kernels: 0 us -> 179 us
  blocking collectives: 153 us -> 0 us
  matrix products: 35.3 us -> 0 us
  starting transfers between devices: 32.8 us -> 0 us
  local copies, waits for them, and re-layouts: 37.3 us -> 9.63 us
  between operations: 17.1 us -> 1.32 us
    psum x1 -> x0, waiting for transfers between devices: 372 us -> none  [shards(): lax.psum((part_self1, part_neigh1, part_self2, part_neigh2, loss_part, co...]
    pallas_call x0 -> x1, Pallas kernels: none -> 179 us  [shards(): pl.pallas_call(kernel, out_shape=[jax.ShapeDtypeStruct((128, 512), f32),...]
    psum x1 -> x0, blocking collectives: 107 us -> none  [shards(): lax.psum((part_self1, part_neigh1, part_self2, part_neigh2, loss_part, co...]
    reduce_scatter x2 -> x0, waiting for transfers between devices: 99.5 us -> none  [the longest x1 51.6 us: shards(): lax.psum_scatter(term_first(jnp.int32(0), lax.axis_size('col') * own_rows...]
    all_gather x1 -> x0, waiting for transfers between devices: 58.4 us -> none  [shards(): group_grads = lax.all_gather(grad_logits, 'col', axis=0, tiled=True)]
    all_to_all x1 -> x0, blocking collectives: 46.1 us -> none  [trade_rows(): lax.all_to_all(outgoing, 'row', split_axis=0, concat_axis=0, tiled=True)]
    all_to_all x2 -> x0, waiting for transfers between devices: 42.7 us -> none  [trade_rows(): lax.all_to_all(outgoing, 'row', split_axis=0, concat_axis=0, tiled=True)]
    dot_general x17 -> x0, matrix products: 35.3 us -> none  [the longest x2 8.67 us: place_rows(): jnp.einsum('tij,tjw->tiw', tile_blocks, source_rows, preferred_element_ty...]
  transfers between devices with their start and end apart: 6 -> 0, of which waited for: 6 -> 0; matrix products, arithmetic and copies ran while one was open for 0% -> 0% of each run, Pallas kernels for 0% -> 0%
where the time goes in v1:
time: 192 us
  Pallas kernels  179 us (93%)
  local copies, waits for them, and re-layouts  9.63 us (5%)
  other arithmetic  2.23 us (1%)
    pallas_call x1, Pallas kernels, shards(): pl.pallas_call(kernel, out_shape=[jax.ShapeDtypeStruct((128, 512), f32),...  179 us
    unnamed x8, local copies, waits for them, and re-layouts  8.39 us

profile of v1, /device:TPU:1, one launch (start us, length us, event | category | flops | bytes accessed | tf_op | source)
XLA Modules:
  0.0 192.0 jit_solution(6800795178502419451)
XLA Ops:
  1.3 0.7 add_bitcast_fusion
  2.0 0.7 select_reduce_fusion.cell
  2.7 1.1 copy.22
  3.7 1.1 copy.23
  4.8 0.9 fusion.2.w2
  5.6 178.8 %sage_step.1 = (f32[128,512]{1,0:T(8,128)}, f32[128,512]{1,0:T(8,128)}, f32[512,172]{1,0:T(8,128)}, f32[512,172]{1,0:T(8,128)}, f32[8,128]{1,0:T(8,128)}) custom-call(s32[384]{0:T(512)} %select_reduce_fusion.cell, bf16[256,128]{1,0:T(8,128)(2,1)} %feat.1, s32[1,2048]{1,0:T(1,128)} %bitcast.11, s32[1,64]{1,0:T(1,128)} %bitcast.14, ...), custom_call_target="tpu_custom_call" | custom-call | tf_op jit(solution)/shard_map/sage_step/pallas_call | solution.py:461
  184.5 0.0 copy-start
  184.5 1.2 slice.3
  185.7 2.0 %copy.24 = f32[512,172]{0,1:T(8,128)} copy(f32[512,172]{1,0:T(8,128)} %get-tuple-element.22) | data formatting | bytes 704512
  187.7 2.0 %copy.25 = f32[512,172]{0,1:T(8,128)} copy(f32[512,172]{1,0:T(8,128)} %get-tuple-element.23) | data formatting | bytes 704512
  189.6 1.7 copy.29
  191.3 0.0 copy-done
  191.3 0.7 copy.30
  (1 shorter events, 0.0 us)
Async XLA Ops:
  184.5 6.8 %copy-start = (f32[128,512]{1,0:T(8,128)S(1)}, f32[128,512]{1,0:T(8,128)}, u32[]{:S(2)}) copy-start(f32[128,512]{1,0:T(8,128)} %get-tuple-element.31) | copy-start | bytes 786436

commit v2 on v1

v2 whole, which is shorter than its diff:
```python
import jax
import jax.numpy as jnp
from jax import lax
from jax.experimental import pallas as pl
from jax.experimental.pallas import tpu as pltpu
from jax.sharding import PartitionSpec as P

MESH = pl.DeviceIdType.MESH
f32, bf16, i32 = jnp.float32, jnp.bfloat16, jnp.int32

NX, NY = 4, 8
NR, NZ = 64, 12
CLASSES = 172
PARTS = 4
TAIL = CLASSES - 128
UP, DOWN = 6, 5


def mm(a, b):
    return jnp.dot(a, b, preferred_element_type=f32)


def mm_t(a, b):
    return lax.dot_general(a, b, (((0,), (0,)), ((), ())), preferred_element_type=f32)


def mm_nt(a, b):
    return lax.dot_general(a, b, (((1,), (1,)), ((), ())), preferred_element_type=f32)


def lanes_of(shape):
    return lax.broadcasted_iota(i32, shape, len(shape) - 1)


def split3(value):
    high = value.astype(bf16).astype(f32)
    middle = (value - high).astype(bf16).astype(f32)
    return high, middle, value - high - middle


def put_scalars(rows, loss, count):
    lanes = lanes_of(rows.shape)
    first = lax.broadcasted_iota(i32, rows.shape, len(rows.shape) - 2) == 0
    for at, part in enumerate(split3(loss) + split3(count)):
        rows = jnp.where(first & (lanes == TAIL + at), part.reshape((1,) * len(rows.shape)), rows)
    return rows


def get_scalars(rows):
    lanes = lanes_of(rows.shape)
    first = lax.broadcasted_iota(i32, rows.shape, 0) == 0

    def total(low):
        live = first & (lanes >= low) & (lanes < low + 3)
        picked = jnp.where(live, rows, 0.0)
        return jnp.sum(jnp.sum(picked, axis=1, keepdims=True), axis=0, keepdims=True)

    return total(TAIL), total(TAIL + 3)


def half_turn(rows):
    return pltpu.roll(rows, 64, axis=1)


def kernel(
    cell, feat, rows, cnt, tiles_hbm, lab, mask, ws1, wn1, ws2t, wn2t,
    fin_out, fin_e_out, sums_out,
    w2t, tiles, dense, pick, s1, r1, s2, r2, s3, r3, wide,
    up_s, up_r, dn_s, dn_r, up2_s, up2_r, dn2_s, dn2_r, gbuf, st, own1, own2,
    pre1, hidden, agg1, gl, sl, neigh, back, mine, pair_r, hs, hr, zs, zr, fin,
    mine_e, pair_e, hs_e, hr_e, zs_e, zr_e, fin_e,
    tile_sem, a1, a2, a3, us, ur, ds, dr, us2, ur2, ds2, dr2, gus, gur, gds, gdr,
    pair_sem, hsem, zsem, fsem, pair2_sem, pair_e_sem, h_e_sem, z_e_sem, f_e_sem, pair2_e_sem,
):
    me = lax.axis_index("row")
    z = lax.axis_index("col")
    core, chip = lax.rem(me, 2), me // 2
    x, y = chip // NY, lax.rem(chip, NY)
    above, below = lax.rem(z + 1, NZ), lax.rem(z + NZ - 1, NZ)
    partner = chip * 2 + 1 - core

    tile_copy = pltpu.make_async_copy(tiles_hbm, tiles.at[pl.ds(0, 64)], tile_sem)
    tile_copy.start()

    barrier = pltpu.get_barrier_semaphore()

    def greet_row(k, c):
        pl.semaphore_signal(barrier, inc=1, device_id=(lax.rem(me + k, NR), z), device_id_type=MESH)
        return c

    def greet_col(k, c):
        pl.semaphore_signal(barrier, inc=1, device_id=(me, lax.rem(z + k, NZ)), device_id_type=MESH)
        return c

    lax.fori_loop(1, NR, greet_row, 0)
    lax.fori_loop(1, NZ, greet_col, 0)

    peer_of = lax.broadcasted_iota(i32, (NR, 2048), 1) // 32 == lax.broadcasted_iota(i32, (NR, 2048), 0)
    counts = jnp.broadcast_to(cnt[...].astype(f32), (8, NR)).astype(bf16)
    live_rows = mm(counts, peer_of.astype(f32).astype(bf16))[0:1]
    place = lax.rem(lax.broadcasted_iota(i32, (1, 2048), 1), 32).astype(f32)
    wanted = jnp.where(place < live_rows, rows[...].astype(f32), -1.0)
    tall = jnp.transpose(jnp.broadcast_to(wanted, (128, 2048)))
    node = lax.broadcasted_iota(i32, (2048, 128), 1).astype(f32)
    pick[:, 0:128] = (tall == node).astype(f32).astype(bf16)
    pick[:, 128:256] = (tall == node + 128.0).astype(f32).astype(bf16)

    pl.semaphore_wait(barrier, NR - 1 + NZ - 1)

    def group_of(dx):
        return lax.rem(x + dx, NX)

    def send_group(dx, src, dst, sem):
        def one(i, c):
            py = lax.rem(y + lax.rem(i // 2 * 3, NY), NY)
            peer = (group_of(dx) * NY + py) * 2 + lax.rem(core + lax.rem(i, 2), 2)
            pltpu.make_async_remote_copy(
                src_ref=src.at[peer], dst_ref=dst.at[me], send_sem=sem.at[0], recv_sem=sem.at[1 + dx],
                device_id=(peer, z), device_id_type=MESH,
            ).start()
            return c

        lax.fori_loop(1 if dx == 0 else 0, 16, one, 0)

    def from_group(dx):
        return lax.rem(x + NX - dx, NX)

    def wait_group(dx, src, dst, sem):
        number = 15 if dx == 0 else 16
        pltpu.make_async_remote_copy(
            src_ref=src.at[pl.ds(0, number)], dst_ref=dst.at[pl.ds(0, number)],
            send_sem=sem.at[0], recv_sem=sem.at[1 + dx], device_id=(partner, z), device_id_type=MESH,
        ).wait_recv()

    def all_of(src, dst, sem, number):
        return pltpu.make_async_remote_copy(
            src_ref=src.at[pl.ds(0, number)], dst_ref=dst.at[pl.ds(0, number)],
            send_sem=sem.at[0], recv_sem=sem.at[1], device_id=(partner, z), device_id_type=MESH,
        )

    def pack_group(dx, value, dst, scalars):
        first = group_of(dx) * 16
        dst[pl.ds(first, 16), 0:32, :] = value[:, 0:128].astype(bf16).reshape(16, 32, 128)
        tail = value[:, 128:256].reshape(16, 2, 16, 128)
        low, high = tail[:, 0], tail[:, 1]
        high = half_turn(high.reshape(256, 128)).reshape(16, 16, 128)
        both = low + high
        if scalars is not None:
            both = put_scalars(both, *scalars)
        dst[pl.ds(first, 16), 32:48, :] = both.astype(bf16)

    def unpack_group(dx, src):
        def one(i, c):
            part = pl.ds(from_group(dx) * 16 + i * 8, 8)
            wide[part, :, 0:128] = src[part, 0:32, :]
            tail = src[part, 32:48, :].astype(f32).reshape(128, 128)
            live = lanes_of((128, 128)) < TAIL
            low = jnp.where(live, tail, 0.0).astype(bf16)
            high = jnp.where(live, half_turn(tail), 0.0).astype(bf16)
            wide[part, 0:16, 128:256] = low.reshape(8, 16, 128)
            wide[part, 16:32, 128:256] = high.reshape(8, 16, 128)
            return c

        lax.fori_loop(0, 2, one, 0)

    order = (2, 1, 3, 0)
    for dx in order:
        at = pl.ds(pl.multiple_of(group_of(dx) * 512, 512), 512)
        block = mm(pick[at, :], feat[...]).astype(bf16)
        s1[pl.ds(group_of(dx) * 16, 16)] = block.reshape(16, 32, 128)
        send_group(dx, s1, r1, a1)
    r1[me] = s1[me]

    w2t[...] = jnp.zeros(w2t.shape, bf16)
    w2t[0:CLASSES] = ws2t[...]
    w2t[256 : 256 + CLASSES] = wn2t[...]

    tile_copy.wait()
    tiles[64] = jnp.zeros((128, 128), bf16)

    def lay(d, c):
        for s in range(16):
            at = pl.ds(pl.multiple_of(d * 128, 128), 128)
            dense[at, s * 128 : (s + 1) * 128] = tiles[cell[d * 16 + s]]
        return c

    lax.fori_loop(0, 24, lay, 0)
    pre1[...] = mm(feat[...], ws1[...])
    up_r[0] = jnp.zeros(up_r.shape[1:], f32)
    dn_r[0] = jnp.zeros(dn_r.shape[1:], f32)
    up2_r[0] = jnp.zeros(up2_r.shape[1:], bf16)
    dn2_r[0] = jnp.zeros(dn2_r.shape[1:], bf16)

    def hop(src, dst, ssem, rsem, j, h, to):
        size = src.shape[1] // PARTS
        part = pl.ds(h * size, size)
        return pltpu.make_async_remote_copy(
            src_ref=src.at[j, part], dst_ref=dst.at[j + 1, part],
            send_sem=ssem.at[j, h], recv_sem=rsem.at[j, h], device_id=(me, to), device_id_type=MESH,
        )

    def ring_sum(chunk, own_part, ups, upr, dns, dnr, uss, urs, dss, drs):
        size = ups.shape[1] // PARTS

        def move(way, h, src, dst, ssem, rsem, j, to):
            part = pl.ds(h * size, size)

            @pl.when(j > 0)
            def _():
                hop(src, dst, ssem, rsem, j - 1, h, to).wait_recv()

            mine_now = own_part[lax.rem(j, 2), way, part]
            src[j, part] = (mine_now + dst[j, part].astype(f32)).astype(src.dtype)
            hop(src, dst, ssem, rsem, j, h, to).start()

        def compute(j):
            own_part[lax.rem(j, 2), 0] = chunk(lax.rem(z + UP - j, NZ))
            own_part[lax.rem(j, 2), 1] = chunk(lax.rem(z + NZ - DOWN + j, NZ))

        def step(j, c):
            for h in range(PARTS):
                if h == PARTS // 2:
                    compute(j + 1)
                move(0, h, ups, upr, uss, urs, j, above)
                move(1, h, dns, dnr, dss, drs, j, below)
            return c

        compute(jnp.int32(0))
        lax.fori_loop(0, DOWN, step, 0)
        last = jnp.int32(DOWN)
        for h in range(PARTS):
            move(0, h, ups, upr, uss, urs, last, above)
        for h in range(PARTS):
            hop(dns, dnr, dss, drs, DOWN - 1, h, below).wait_recv()
        for h in range(PARTS):
            hop(ups, upr, uss, urs, UP - 1, h, above).wait_recv()
        return own_part[DOWN % 2, 1] + dnr[DOWN].astype(f32) + upr[UP].astype(f32)

    def ring_sent(ups, upr, dns, dnr, uss, urs, dss, drs):
        def sent(j, c):
            for h in range(PARTS):
                hop(ups, upr, uss, urs, j, h, above).wait_send()

                @pl.when(j < DOWN)
                def _():
                    hop(dns, dnr, dss, drs, j, h, below).wait_send()

            return c

        lax.fori_loop(0, UP, sent, 0)

    def block_rows(o):
        return dense[pl.ds(pl.multiple_of(o * 256, 256), 256), :]

    for dx in order:
        wait_group(dx, s1, r1, a1)

    def chunk1(o):
        return mm(block_rows(o), r1[...].reshape(2048, 128))

    ring1 = (up_s, up_r, dn_s, dn_r, us, ur, ds, dr)
    agg1[...] = ring_sum(chunk1, own1, *ring1).astype(bf16)

    pre = pre1[...] + mm(agg1[...], wn1[...])
    pre1[...] = pre
    hidden[...] = jnp.maximum(pre, 0.0).astype(bf16)
    neigh[...] = mm_nt(hidden[...], w2t[256:512]).astype(bf16)

    for dx in order:
        at = pl.ds(pl.multiple_of(group_of(dx) * 512, 512), 512)
        pack_group(dx, mm(pick[at, :], neigh[...]), s2, None)
        send_group(dx, s2, r2, a2)
    r2[me] = s2[me]
    sl[...] = mm_nt(hidden[...], w2t[0:256])
    ring_sent(*ring1)
    all_of(s1, r1, a1, NR - 1).wait_send()
    for dx in order:
        wait_group(dx, s2, r2, a2)
        unpack_group(dx, r2)

    def pack_chunk(full):
        tail = full[:, 128:256]
        both = tail[0:128] + half_turn(tail[128:256])
        return jnp.concatenate([full[:, 0:128], both], axis=0)

    def unpack_chunk(packed):
        tail = packed[256:384]
        live = lanes_of((128, 128)) < TAIL
        low = jnp.where(live, tail, 0.0)
        high = jnp.where(live, half_turn(tail), 0.0)
        return jnp.concatenate([packed[0:256], jnp.concatenate([low, high], axis=0)], axis=1)

    def chunk2(o):
        return pack_chunk(mm(block_rows(o), wide[...].reshape(2048, 256)))

    ring2 = (up2_s, up2_r, dn2_s, dn2_r, us2, ur2, ds2, dr2)
    agg2 = unpack_chunk(ring_sum(chunk2, own2, *ring2)).astype(bf16).astype(f32)

    logits = sl[...] + agg2
    lanes = lanes_of((256, 256))
    live = lanes < CLASSES

    def tall_of(ref):
        one = jnp.transpose(jnp.broadcast_to(ref[...].astype(f32), (128, 256)))
        return jnp.concatenate([one, one], axis=1)

    hit = lanes.astype(f32) == tall_of(lab)
    train = tall_of(mask)
    log_total = jnp.log(jnp.sum(jnp.where(live, jnp.exp(logits), 0.0), axis=1, keepdims=True))
    cross = log_total - jnp.sum(jnp.where(hit, logits, 0.0), axis=1, keepdims=True)
    prob = jnp.where(live, jnp.exp(logits - log_total), 0.0)
    grad = (train * (prob - hit.astype(f32))).astype(bf16)
    gl[...] = grad
    loss_part = jnp.sum(train[:, 0:1] * cross, axis=0, keepdims=True)
    count_part = jnp.sum(train[:, 0:1], axis=0, keepdims=True)

    def fill(buf, number, parts):
        for b in range(4):
            cut = jnp.concatenate([part[:, b * 128 : (b + 1) * 128] for part in parts], axis=0)
            buf[b * 16 : (b + 1) * 16] = cut.reshape(16, number, 128)

    def to_pair(src, dst, sem, first_s, first_d):
        return pltpu.make_async_remote_copy(
            src_ref=src.at[pl.ds(first_s, 32)], dst_ref=dst.at[pl.ds(first_d, 32)],
            send_sem=sem.at[0], recv_sem=sem.at[1], device_id=(partner, z), device_id_type=MESH,
        )

    def chip_at(dx, k):
        return group_of(dx) * NY + lax.rem(y + k * 3, NY)

    def plane_send(src, dst, sem):
        for dx in range(NX):

            def one(k, c):
                other = chip_at(dx, k)
                pltpu.make_async_remote_copy(
                    src_ref=src.at[other], dst_ref=dst.at[chip], send_sem=sem.at[0], recv_sem=sem.at[1],
                    device_id=(other * 2 + core, z), device_id_type=MESH,
                ).start()
                return c

            lax.fori_loop(1 if dx == 0 else 0, NY, one, 0)

    def plane_gather(buf, sem):
        for dx in range(NX):

            def one(k, c):
                pltpu.make_async_remote_copy(
                    src_ref=buf.at[piece], dst_ref=buf.at[piece], send_sem=sem.at[0], recv_sem=sem.at[1 + dx],
                    device_id=(chip_at(dx, k) * 2 + core, z), device_id_type=MESH,
                ).start()
                return c

            lax.fori_loop(1 if dx == 0 else 0, NY, one, 0)

    def pair_gather(buf, sem, pair_sems):
        copies = []
        for dx in range(NX):
            number = NY - 1 if dx == 0 else NY
            pltpu.make_async_remote_copy(
                src_ref=buf.at[pl.ds(0, number)], dst_ref=buf.at[pl.ds(0, number)],
                send_sem=sem.at[0], recv_sem=sem.at[1 + dx], device_id=(partner, z), device_id_type=MESH,
            ).wait_recv()
            part = pl.ds(core * 32 + from_group(dx) * NY, NY)
            copies.append(pltpu.make_async_remote_copy(
                src_ref=buf.at[part], dst_ref=buf.at[part],
                send_sem=pair_sems.at[dx, 0], recv_sem=pair_sems.at[dx, 1],
                device_id=(partner, z), device_id_type=MESH,
            ))
            copies[-1].start()
        return copies

    def plane_scatter(buf, got, hs, hr, sem):
        hs[...] = (buf[pl.ds(core * 32, 32)] + got[...]).astype(bf16)
        plane_send(hs, hr, sem)
        hr[chip] = hs[chip]

    def col_send(zs, zr, sem):
        def one(k, c):
            pltpu.make_async_remote_copy(
                src_ref=zs, dst_ref=zr.at[z], send_sem=sem.at[0], recv_sem=sem.at[1],
                device_id=(me, lax.rem(z + k, NZ)), device_id_type=MESH,
            ).start()
            return c

        lax.fori_loop(1, NZ, one, 0)
        zr[z] = zs[...]

    def summed(buf):
        return jnp.sum(buf[...].astype(f32), axis=0).astype(bf16)

    piece = core * 32 + chip

    packed = pack_chunk(grad.astype(f32))
    gbuf[z, 0:256] = packed[0:256].astype(bf16)
    gbuf[z, 256:384] = put_scalars(packed[256:384], loss_part, count_part).astype(bf16)

    def pass_on(owner, ssem, rsem, j, h, to):
        part = pl.ds(h * (384 // PARTS), 384 // PARTS)
        return pltpu.make_async_remote_copy(
            src_ref=gbuf.at[owner, part], dst_ref=gbuf.at[owner, part],
            send_sem=ssem.at[j, h], recv_sem=rsem.at[j, h], device_id=(me, to), device_id_type=MESH,
        )

    def up_hop(j, h):
        return pass_on(lax.rem(z + NZ - j, NZ), gus, gur, j, h, above)

    def down_hop(j, h):
        return pass_on(lax.rem(z + j, NZ), gds, gdr, j, h, below)

    def back_chunk(o):
        full = unpack_chunk(gbuf[o].astype(f32))
        return mm(jnp.transpose(full).astype(bf16), block_rows(o))

    for h in range(PARTS):
        up_hop(0, h).start()
        down_hop(0, h).start()
    fill(mine_e, 16, (mm_t(gl[...], hidden[...]),))
    swap_e = to_pair(mine_e, pair_e, pair_e_sem, (1 - core) * 32, 0)
    swap_e.start()
    st[...] = back_chunk(z)

    def both_ways(j, h):
        up_hop(j - 1, h).wait_recv()
        up_hop(j, h).start()
        down_hop(j - 1, h).wait_recv()

        @pl.when(j < DOWN)
        def _():
            down_hop(j, h).start()

    def add_chunks(j):
        st[...] += back_chunk(lax.rem(z + NZ - j, NZ)) + back_chunk(lax.rem(z + j, NZ))

    def gather_step(j, c):
        for h in range(PARTS // 2):
            both_ways(j, h)

        @pl.when(j > 1)
        def _():
            add_chunks(j - 1)

        for h in range(PARTS // 2, PARTS):
            both_ways(j, h)
        return c

    lax.fori_loop(1, 2, gather_step, 0)
    swap_e.wait_recv()
    plane_scatter(mine_e, pair_e, hs_e, hr_e, h_e_sem)
    lax.fori_loop(2, UP, gather_step, 0)
    add_chunks(UP - 1)
    for h in range(PARTS):
        up_hop(UP - 1, h).wait_recv()
    st[...] += back_chunk(lax.rem(z + NZ - UP, NZ))
    col_sums = get_scalars(jnp.sum(gbuf[:, 256:272, :].astype(f32), axis=0))

    for dx in order:
        at = pl.ds(pl.multiple_of(group_of(dx) * 512, 512), 512)
        pack_group(dx, jnp.transpose(st[:, at]), s3, col_sums)
        send_group(dx, s3, r3, a3)
    r3[me] = s3[me]

    all_of(hs_e, hr_e, h_e_sem, 31).wait_recv()
    zs_e[...] = summed(hr_e)
    col_send(zs_e, zr_e, z_e_sem)
    swap_e.wait_send()
    all_of(hs_e, hr_e, h_e_sem, 31).wait_send()
    ring_sent(*ring2)

    def gather_sent(j, c):
        for h in range(PARTS):
            up_hop(j, h).wait_send()

            @pl.when(j < DOWN)
            def _():
                down_hop(j, h).wait_send()

        return c

    lax.fori_loop(0, UP, gather_sent, 0)
    all_of(s2, r2, a2, NR - 1).wait_send()
    all_of(zr_e, zr_e, z_e_sem, NZ - 1).wait_recv()
    fin_e[piece] = summed(zr_e)
    total = jnp.zeros((256, 256), f32)
    for dx in order:
        wait_group(dx, s3, r3, a3)
        if dx == order[-1]:
            plane_gather(fin_e, f_e_sem)
        unpack_group(dx, r3)
        at = pl.ds(pl.multiple_of(from_group(dx) * 512, 512), 512)
        rows_at = wide[pl.ds(from_group(dx) * 16, 16)].reshape(512, 256)
        total = total + mm_t(pick[at, :], rows_at)
    back[...] = total.astype(bf16)
    loss_sum, node_count = get_scalars(jnp.sum(r3[:, 32:48, :].astype(f32), axis=0))

    grad_hidden = mm(gl[...], w2t[0:256]) + mm(back[...], w2t[256:512])
    grad_pre = jnp.where(pre1[...] > 0, grad_hidden, 0.0).astype(bf16)
    parts = (
        mm_t(feat[...], grad_pre),
        mm_t(agg1[...], grad_pre),
        mm_t(back[...], hidden[...]),
    )
    fill(mine, 32, parts)
    swap = to_pair(mine, pair_r, pair_sem, (1 - core) * 32, 0)
    swap.start()
    swap.wait_recv()
    plane_scatter(mine, pair_r, hs, hr, hsem)
    all_of(s3, r3, a3, NR - 1).wait_send()
    swap.wait_send()
    all_of(zr_e, zr_e, z_e_sem, NZ - 1).wait_send()
    swaps_e = pair_gather(fin_e, f_e_sem, pair2_e_sem)
    all_of(hs, hr, hsem, 31).wait_recv()
    zs[...] = summed(hr)
    col_send(zs, zr, zsem)
    all_of(hs, hr, hsem, 31).wait_send()
    all_of(fin_e, fin_e, f_e_sem, 31).wait_send()
    all_of(zr, zr, zsem, NZ - 1).wait_recv()
    fin[piece] = summed(zr)
    plane_gather(fin, fsem)
    for copy in swaps_e:
        copy.wait_recv()
    fin_e_out[...] = fin_e[...]
    all_of(zr, zr, zsem, NZ - 1).wait_send()
    swaps = pair_gather(fin, fsem, pair2_sem)

    lanes = lanes_of((8, 128))
    sums_out[...] = jnp.where(lanes == 0, loss_sum, jnp.where(lanes == 1, node_count, 0.0))
    for copy in swaps:
        copy.wait_recv()
    fin_out[...] = fin[...]
    for copy in swaps + swaps_e:
        copy.wait_send()
    all_of(fin, fin, fsem, 31).wait_send()


def finish(fin, fin_e, sums, g1, g2, g3t, g4t, loss):
    loss_sum, node_count = sums[0:1, 0:1], jnp.maximum(sums[0:1, 1:2], 1.0)
    loss[...] = loss_sum / node_count
    scale = 1.0 / jnp.sqrt(node_count)
    for b in range(4):
        at = slice(b * 128, (b + 1) * 128)
        cut = fin[b * 16 : (b + 1) * 16].astype(f32).reshape(512, 128) * scale
        cut_e = fin_e[b * 16 : (b + 1) * 16].astype(f32).reshape(256, 128) * scale
        g1[:, at] = cut[0:128]
        g2[:, at] = cut[128:256]
        g3t[:, at] = cut_e[0:CLASSES]
        g4t[:, at] = cut[256 : 256 + CLASSES]


def shards(
    features, send_rows, send_count, tile_values, tile_dst, tile_src, tile_count,
    labels, train_mask, w_self1, w_neigh1, w_self2, w_neigh2,
):
    slots = jnp.arange(64, dtype=i32)
    where = tile_dst.reshape(1, 64) * 16 + tile_src.reshape(1, 64)
    here = (jnp.arange(384, dtype=i32)[:, None] == where) & (slots < tile_count.reshape(()))[None, :]
    cell = jnp.min(jnp.where(here, slots[None, :], 64), axis=1)
    vm = pl.BlockSpec(memory_space=pltpu.VMEM)
    sm = pl.BlockSpec(memory_space=pltpu.SMEM)
    V = pltpu.VMEM
    dma = pltpu.SemaphoreType.DMA
    fin, fin_e, sums = pl.pallas_call(
        kernel,
        out_shape=[
            jax.ShapeDtypeStruct((64, 32, 128), bf16),
            jax.ShapeDtypeStruct((64, 16, 128), bf16),
            jax.ShapeDtypeStruct((8, 128), f32),
        ],
        in_specs=[sm, vm, vm, vm, pl.BlockSpec(memory_space=pl.ANY), vm, vm, vm, vm, vm, vm],
        out_specs=[vm] * 3,
        scratch_shapes=[
            V((512, 512), bf16),
            V((65, 128, 128), bf16),
            V((3072, 2048), bf16),
            V((2048, 256), bf16),
            V((64, 32, 128), bf16), V((64, 32, 128), bf16),
            V((64, 48, 128), bf16), V((64, 48, 128), bf16),
            V((64, 48, 128), bf16), V((64, 48, 128), bf16),
            V((64, 32, 256), bf16),
            V((UP, 256, 128), f32), V((UP + 1, 256, 128), f32),
            V((DOWN, 256, 128), f32), V((DOWN + 1, 256, 128), f32),
            V((UP, 384, 128), bf16), V((UP + 1, 384, 128), bf16),
            V((DOWN, 384, 128), bf16), V((DOWN + 1, 384, 128), bf16),
            V((NZ, 384, 128), bf16),
            V((256, 2048), f32),
            V((2, 2, 256, 128), f32), V((2, 2, 384, 128), f32),
            V((256, 512), f32),
            V((256, 512), bf16),
            V((256, 128), bf16),
            V((256, 256), bf16),
            V((256, 256), f32),
            V((256, 256), bf16),
            V((256, 256), bf16),
            V((64, 32, 128), f32), V((32, 32, 128), f32),
            V((32, 32, 128), bf16), V((32, 32, 128), bf16),
            V((32, 128), bf16), V((NZ, 32, 128), bf16),
            V((64, 32, 128), bf16),
            V((64, 16, 128), f32), V((32, 16, 128), f32),
            V((32, 16, 128), bf16), V((32, 16, 128), bf16),
            V((16, 128), bf16), V((NZ, 16, 128), bf16),
            V((64, 16, 128), bf16),
            dma, dma((1 + NX,)), dma((1 + NX,)), dma((1 + NX,)),
            dma((UP, PARTS)), dma((UP, PARTS)), dma((DOWN, PARTS)), dma((DOWN, PARTS)),
            dma((UP, PARTS)), dma((UP, PARTS)), dma((DOWN, PARTS)), dma((DOWN, PARTS)),
            dma((UP, PARTS)), dma((UP, PARTS)), dma((DOWN, PARTS)), dma((DOWN, PARTS)),
            dma((2,)), dma((2,)), dma((2,)), dma((1 + NX,)), dma((NX, 2)),
            dma((2,)), dma((2,)), dma((2,)), dma((1 + NX,)), dma((NX, 2)),
        ],
        compiler_params=pltpu.CompilerParams(
            collective_id=0, has_side_effects=True, vmem_limit_bytes=56 * 1024 * 1024
        ),
        name="sage_step",
    )(
        cell, features, send_rows.reshape(1, 2048), send_count.reshape(1, 64),
        tile_values.reshape(64, 128, 128), labels.reshape(1, 256), train_mask.reshape(1, 256),
        w_self1, w_neigh1, w_self2.T, w_neigh2.T,
    )
    g1, g2, g3t, g4t, loss = pl.pallas_call(
        finish,
        out_shape=[
            jax.ShapeDtypeStruct((128, 512), f32),
            jax.ShapeDtypeStruct((128, 512), f32),
            jax.ShapeDtypeStruct((CLASSES, 512), f32),
            jax.ShapeDtypeStruct((CLASSES, 512), f32),
            jax.ShapeDtypeStruct((1, 1), f32),
        ],
        in_specs=[vm] * 3,
        out_specs=[vm] * 5,
        compiler_params=pltpu.CompilerParams(vmem_limit_bytes=56 * 1024 * 1024),
        name="sage_finish",
    )(fin, fin_e, sums)
    return g1, g2, g3t.T, g4t.T, loss.reshape(())


def solution(mesh):
    in_specs = (
        P(("row", "col"), None),
        P("row", "col", None),
        P("row", "col", None),
        P("row", "col", None, None, None),
        P("row", "col", None),
        P("row", "col", None),
        P("row", "col"),
        P(("row", "col")),
        P(("row", "col")),
        P(),
        P(),
        P(),
        P(),
    )
    out_specs = (P(), P(), P(), P(), P())
    return jax.shard_map(shards, mesh=mesh, in_specs=in_specs, out_specs=out_specs, check_vma=False)
```

time: 192 us -> 174 us (0.906)
  local copies, waits for them, and re-layouts: 9.63 us -> 0 us
  Pallas kernels: 179 us -> 171 us
    unnamed x8 -> x0, local copies, waits for them, and re-layouts: 8.39 us -> none
    pallas_call x1 -> x2, Pallas kernels: 179 us -> 171 us  [the longest x1 169 us: shards(): pl.pallas_call(kernel, out_shape=[jax.ShapeDtypeStruct((64, 32, 128), bf1...]
where the time goes in v2:
time: 174 us
  Pallas kernels  171 us (98%)
    pallas_call x1, Pallas kernels, shards(): pl.pallas_call(kernel, out_shape=[jax.ShapeDtypeStruct((64, 32, 128), bf1...  169 us

profile of v2, /device:TPU:1, one launch (start us, length us, event | category | flops | bytes accessed | tf_op | source)
XLA Modules:
  0.0 173.6 jit_solution(8148182646528160956)
XLA Ops:
  1.3 0.7 add_bitcast_fusion
  2.0 0.7 select_reduce_fusion.cell
  2.7 168.6 %sage_step.1 = (bf16[64,32,128]{2,1,0:T(8,128)(2,1)}, bf16[64,16,128]{2,1,0:T(8,128)(2,1)}, f32[8,128]{1,0:T(8,128)}) custom-call(s32[384]{0:T(512)} %select_reduce_fusion.cell, bf16[256,128]{1,0:T(8,128)(2,1)} %feat.1, s32[1,2048]{1,0:T(1,128)} %bitcast.17, s32[1,64]{1,0:T(1,128)} %bitcast.20, bf16[64,128,128]{2,1,0:T(8,128)(2,1)} %bitcast.14, ...), custom_call_target="tpu_custom_call" | custom-call | tf_op jit(solution)/shard_map/sage_step/pallas_call | solution.py:562
  171.3 2.3 %sage_finish.1 = (f32[128,512]{1,0:T(8,128)}, f32[128,512]{1,0:T(8,128)}, f32[172,512]{1,0:T(8,128)}, f32[172,512]{1,0:T(8,128)}, f32[1,1]{1,0:T(1,128)}) custom-call(bf16[64,32,128]{2,1,0:T(8,128)(2,1)} %get-tuple-element.13.fin, bf16[64,16,128]{2,1,0:T(8,128)(2,1)} %get-tuple-element.14.fin_e, f32[8,128]{1,0:T(8,128)} %get-tuple-element.15.sums), custom_call_target="tpu_custom_call" | custom-call | tf_op jit(solution)/shard_map/sage_finish/pallas_call | solution.py:618
  (1 shorter events, 0.0 us)
